TPU v7x, 32 devices: a whole 2x2x4 slice. The times are simulated.
32 devices in a mesh: groups: 2 (over x), shard: 16 (over z, y, core).
Axes of the slice: x: 2, y: 2, z: 4, core: 2. Of those that a mesh axis runs over, the one named last changes fastest.
Arguments:
- kv_store: bfloat16 [64, 256, 2048], P(('groups', 'shard')), parts along dimension 0, may hold values from -6 to 6
- block_order: int32 [64], P(('groups', 'shard')), parts along dimension 0, may hold values from 0 to 31, as said below
- lengths: int32 [16], P('groups'), parts along dimension 0, may hold values from 1 to 12, as said below
- row_positions: int32 [16, 128], P('groups'), parts along dimension 0, may hold values from 0 to 3071, as said below
- queries: bfloat16 [256, 65536], P('groups', 'shard'), parts along dimension 0, may hold values from -48 to 48
- fresh_rows: bfloat16 [256, 16384], P('groups', 'shard'), parts along dimension 0, may hold values from -280 to 280
Outputs:
- attended: bfloat16 [256, 65536], P('groups', 'shard'), parts along dimension 0
There are 2 independent parts, one for each index of `groups`. A program takes and returns all parts, laid end to end along the dimension named above; each array names one. Nothing has to cross between parts.
Inputs may be any that keep to these rules, and one draw needn't show every extreme that they name: Each request has at least one block, the lengths sum to 32, and the longest request has exactly 12 blocks. Request r and request r + 4 together have at most 16 blocks, exactly so for the pair of the longest request. `row_positions`: each request's positions are non-decreasing and lie below 256 times its length; its last recomputed row is its last token, 256 lengths[r] - 1. `block_order`: A permutation; the 2 slots of one device (slots 2 d to 2 d + 1) hold blocks of requests r1, r2 with r1 % (4) != r2 % 4.
All inputs are finite; a program needn't handle non-finite values.
Results may differ from a plain program's by a relative error of at most 0.0041.
Values may be sent and summed in bfloat16 or wider, within the bound.
A program may use at most 64 MiB of HBM per device.

v0:
```python
import functools
import math

import jax
import jax.numpy as jnp
from jax import lax
from jax.experimental import pallas as pl
from jax.experimental.pallas import tpu as pltpu
from jax.sharding import PartitionSpec as P

QH = 64
KVH = 8
HD = 128
REQS = 8
GROUP = QH // KVH
PAIRS = REQS // 2

ROPE_BASE = 500000.0
NEG_FILL = -1e30
NEG_START = -1e29
LOG2E = 1.4426950408889634
NT = (((1,), (1,)), ((), ()))
TN = (((0,), (0,)), ((), ()))


def frequencies(half_size):
    step_ids = jnp.arange(half_size, dtype=jnp.float32)
    return jnp.exp(-math.log(ROPE_BASE) * step_ids / half_size)


def turn_tables(positions):
    angle = positions.astype(jnp.float32)[..., None] * frequencies(HD // 2)
    cosine, sine = jnp.cos(angle), jnp.sin(angle)
    return (
        jnp.concatenate([cosine, cosine], axis=-1),
        jnp.concatenate([-sine, sine], axis=-1),
    )


def turned(x, cosine, sine):
    x = x.astype(jnp.float32)
    return (x * cosine + pltpu.roll(x, HD // 2, 1) * sine).astype(jnp.bfloat16)


def lookup(values, table_ids, where_at):
    return jnp.sum(jnp.where(where_at[..., None] == table_ids, values, 0), axis=-1)


def whole_kernel(
    n,
    scale,
    sel_ref,
    kv_ref,
    bcos_ref,
    bsin_ref,
    meta_ref,
    q_ref,
    fresh_ref,
    cos_ref,
    sin_ref,
    limit_ref,
    req_ref,
    out_ref,
    sent,
    received,
    metas,
    partner_q,
    qs,
    top,
    total,
    acc,
    o0,
    lse0,
    o1,
    lse1,
    o1_in,
    lse1_in,
    kv_send,
    kv_recv,
    meta_send,
    meta_recv,
    q_send,
    q_recv,
    o_send,
    o_recv,
    l_send,
    l_recv,
    local_sem,
):
    heads, peers, block_len, _ = sent.shape
    rows = q_ref.shape[0]
    lanes = rows * GROUP
    q_width = GROUP * HD
    per_req = n // REQS
    device = lax.axis_index("shard")
    me = lax.rem(device, peers)
    first_peer = device - me
    partner = lax.rem(device + peers, n)
    log_scale = scale * LOG2E

    def remote(src, dst, send, recv, target):
        return pltpu.make_async_remote_copy(
            src_ref=src,
            dst_ref=dst,
            send_sem=send,
            recv_sem=recv,
            device_id={"shard": target},
            device_id_type=pl.DeviceIdType.MESH,
        )

    def kv_copy(c, i, slot):
        return remote(sent.at[c, i], received.at[c, slot], kv_send.at[c, i], kv_recv.at[c, slot], first_peer + i)

    def meta_copy(i, slot):
        return remote(
            meta_ref.at[i // per_req], metas.at[slot], meta_send.at[i], meta_recv.at[slot], first_peer + i
        )

    def q_copy(c):
        columns = pl.ds(pl.multiple_of(c * q_width, q_width), q_width)
        return remote(q_ref.at[:, columns], partner_q.at[c], q_send.at[c], q_recv.at[c], partner)

    def o_copy(c):
        return remote(o1.at[c], o1_in.at[c], o_send.at[c], o_recv.at[c], partner)

    def l_copy(c):
        return remote(lse1.at[c], lse1_in.at[c], l_send.at[c], l_recv.at[c], partner)

    def own_kv(c):
        return pltpu.make_async_copy(sent.at[c, me], received.at[c, me], local_sem.at[c])

    barrier = pltpu.get_barrier_semaphore()
    pl.semaphore_signal(barrier, inc=1, device_id={"shard": partner}, device_id_type=pl.DeviceIdType.MESH)

    def greet(t, carry):
        pl.semaphore_signal(
            barrier,
            inc=1,
            device_id={"shard": first_peer + lax.rem(me + t, peers)},
            device_id_type=pl.DeviceIdType.MESH,
        )
        return carry

    lax.fori_loop(1, peers, greet, 0)
    pl.semaphore_wait(barrier, peers)

    own_meta = pltpu.make_async_copy(meta_ref.at[me // per_req], metas.at[me], local_sem.at[heads])
    own_meta.start()

    def tell(t, carry):
        meta_copy(lax.rem(me + t, peers), me).start()
        return carry

    lax.fori_loop(1, peers, tell, 0)

    def pack_chunk(c, carry):
        q_copy(c).start()

        def pack(t, carry):
            i = lax.rem(me + t, peers)
            pair, group = i // per_req, lax.rem(i, per_req)
            sel = sel_ref[pair]
            column = pl.multiple_of((group * heads + c) * 2 * HD, 2 * HD)
            key = kv_ref[sel, :, pl.ds(column, HD)]
            sent[c, i, :, pl.ds(0, HD)] = turned(key, bcos_ref[sel], bsin_ref[sel])
            sent[c, i, :, pl.ds(HD, HD)] = kv_ref[sel, :, pl.ds(pl.multiple_of(column + HD, HD), HD)]

            @pl.when(t > 0)
            def _():
                kv_copy(c, i, me).start()

            @pl.when(t == 0)
            def _():
                own_kv(c).start()

            return carry

        return lax.fori_loop(0, peers, pack, carry)

    lax.fori_loop(0, heads, pack_chunk, 0)

    def hear(t, carry):
        j = lax.rem(me + t, peers)
        meta_copy(j, j).wait_recv()
        return carry

    own_meta.wait()
    lax.fori_loop(1, peers, hear, 0)

    def attend_chunk(c, carry):
        q_copy(c).wait_recv()
        f_column = pl.multiple_of(c * 2 * HD, 2 * HD)
        for g in range(GROUP):
            own_rows = pl.ds(g * rows, rows)
            column = pl.multiple_of(c * q_width + g * HD, HD)
            qs[0, own_rows, :] = turned(q_ref[:, pl.ds(column, HD)], cos_ref[0], sin_ref[0])
            qs[1, own_rows, :] = turned(partner_q[c, :, pl.ds(g * HD, HD)], cos_ref[1], sin_ref[1])
        own_key = turned(fresh_ref[:, pl.ds(f_column, HD)], cos_ref[0], sin_ref[0])
        own = lax.dot_general(own_key, qs[0], NT, preferred_element_type=jnp.float32)
        row_of = lax.broadcasted_iota(jnp.int32, (rows, lanes), 0)
        lane_of = lax.broadcasted_iota(jnp.int32, (rows, lanes), 1) % rows
        top[0] = jnp.sum(jnp.where(row_of == lane_of, own, 0.0), axis=0, keepdims=True)
        total[0] = jnp.ones((1, lanes), jnp.float32)
        own_value = fresh_ref[:, pl.ds(pl.multiple_of(f_column + HD, HD), HD)].astype(jnp.float32).T
        for g in range(GROUP):
            acc[0, :, pl.ds(g * rows, rows)] = own_value
        top[1] = jnp.full((1, lanes), NEG_START, jnp.float32)
        total[1] = jnp.zeros((1, lanes), jnp.float32)
        acc[1] = jnp.zeros((HD, lanes), jnp.float32)

        def attend(t, carry):
            j = lax.rem(me + peers - t, peers)

            @pl.when(t > 0)
            def _():
                kv_copy(c, j, j).wait_recv()

            @pl.when(t == 0)
            def _():
                own_kv(c).wait()

            req = metas[j, 0:1, :]
            offset = metas[j, 1:2, :]
            is_own = req == req_ref[0:1, :]
            is_partner = req == req_ref[1:2, :]
            pick0 = jnp.where(is_own, 1.0, 0.0).astype(jnp.bfloat16)
            pick1 = jnp.where(is_own, 0.0, 1.0).astype(jnp.bfloat16)
            query = qs[0] * pick0 + qs[1] * pick1
            wide_own = jnp.concatenate([is_own.astype(jnp.int32)] * GROUP, axis=1) > 0
            wide_partner = jnp.concatenate([is_partner.astype(jnp.int32)] * GROUP, axis=1) > 0
            wide_offset = jnp.concatenate([offset] * GROUP, axis=1)
            limit = jnp.where(wide_own, limit_ref[0], limit_ref[1]) - wide_offset
            keys = received[c, j, :, pl.ds(0, HD)]
            values = received[c, j, :, pl.ds(HD, HD)]
            scores = lax.dot_general(keys, query, NT, preferred_element_type=jnp.float32)
            token = lax.broadcasted_iota(jnp.int32, scores.shape, 0)
            scores = jnp.where(token < limit, scores, NEG_FILL)
            block_top = jnp.max(scores, axis=0, keepdims=True)
            weights = jnp.exp2((scores - block_top) * log_scale).astype(jnp.bfloat16)
            block_sum = jnp.sum(weights.astype(jnp.float32), axis=0, keepdims=True)
            block_out = lax.dot_general(values, weights, TN, preferred_element_type=jnp.float32)
            for side, chosen in enumerate((wide_own, wide_partner)):
                old_top = top[side]
                new_top = jnp.where(chosen, jnp.maximum(old_top, block_top), old_top)
                old_factor = jnp.exp2((old_top - new_top) * log_scale)
                new_factor = jnp.where(
                    chosen, jnp.exp2(jnp.where(chosen, block_top - new_top, 0.0) * log_scale), 0.0
                )
                top[side] = new_top
                total[side] = total[side] * old_factor + block_sum * new_factor
                acc[side] = acc[side] * old_factor + block_out * new_factor
            return carry

        lax.fori_loop(0, peers, attend, 0)
        o0[c] = acc[0] * (1.0 / total[0])
        lse0[c] = top[0] * scale + jnp.log(total[0])
        some = total[1] > 0.0
        safe = jnp.where(some, total[1], 1.0)
        o1[c] = (acc[1] * (1.0 / safe)).astype(jnp.bfloat16)
        sent_lse = jnp.where(some, top[1] * scale + jnp.log(safe), NEG_FILL)
        for g in range(GROUP):
            lse1[c, g : g + 1, :] = sent_lse[:, g * rows : (g + 1) * rows]
        l_copy(c).start()
        o_copy(c).start()
        return carry

    lax.fori_loop(0, heads, attend_chunk, 0)

    def merge_chunk(c, carry):
        l_copy(c).wait_recv()
        o_copy(c).wait_recv()
        base = lse0[c]
        other = jnp.concatenate([lse1_in[c, g : g + 1, :] for g in range(GROUP)], axis=1)
        larger = jnp.maximum(base, other)
        first, second = jnp.exp(base - larger), jnp.exp(other - larger)
        scaled = 1.0 / (first + second)
        joined = o0[c] * (first * scaled) + o1_in[c].astype(jnp.float32) * (second * scaled)
        for g in range(GROUP):
            column = pl.multiple_of(c * q_width + g * HD, HD)
            out_ref[:, pl.ds(column, HD)] = joined[:, g * rows : (g + 1) * rows].T.astype(out_ref.dtype)
        return carry

    lax.fori_loop(0, heads, merge_chunk, 0)

    def finish(c, carry):
        def sent_kv(t, carry):
            kv_copy(c, lax.rem(me + t, peers), me).wait_send()
            return carry

        lax.fori_loop(1, peers, sent_kv, 0)
        q_copy(c).wait_send()
        o_copy(c).wait_send()
        l_copy(c).wait_send()
        return carry

    lax.fori_loop(0, heads, finish, 0)

    def told(t, carry):
        meta_copy(lax.rem(me + t, peers), me).wait_send()
        return carry

    lax.fori_loop(1, peers, told, 0)


def shards(kv_store, block_order, lengths, row_positions, queries, fresh_rows):
    n_shard = lax.axis_size("shard")
    peers = n_shard // 2
    per_req = n_shard // REQS
    blk_dev, block_len, width = kv_store.shape
    heads = width // (per_req * 2 * HD)
    rows = queries.shape[0]
    lanes = rows * GROUP
    my_req = lax.axis_index("shard") // per_req
    req_ids = jnp.arange(REQS, dtype=jnp.int32)
    starts = jnp.sum(jnp.where(req_ids[None, :] < req_ids[:, None], lengths[None, :], 0), axis=1)
    dest = jnp.sum((block_order[:, None] >= starts[None, 1:]).astype(jnp.int32), axis=-1)
    offset = (block_order - lookup(starts, req_ids, dest)) * block_len
    pair_ids = jnp.arange(PAIRS, dtype=jnp.int32)
    slot_ids = jnp.arange(blk_dev, dtype=jnp.int32)
    for_pair = (dest % PAIRS)[None, :] == pair_ids[:, None]
    sel = jnp.sum(jnp.where(for_pair, slot_ids[None, :], 0), axis=1)
    pair_req = jnp.sum(jnp.where(for_pair, dest[None, :] + 1, 0), axis=1) - 1
    pair_offset = jnp.sum(jnp.where(for_pair, offset[None, :], 0), axis=1)
    row_ids = jnp.arange(8, dtype=jnp.int32)
    meta = jnp.broadcast_to(
        jnp.where(row_ids[None, :] == 0, pair_req[:, None], pair_offset[:, None])[:, :, None], (PAIRS, 8, HD)
    )
    block_cos, block_sin = turn_tables(offset[:, None])
    other_req = (my_req + PAIRS) % REQS
    both = jnp.stack(
        [
            lax.dynamic_index_in_dim(row_positions, my_req, 0, keepdims=False),
            lax.dynamic_index_in_dim(row_positions, other_req, 0, keepdims=False),
        ]
    )
    row_cos, row_sin = turn_tables(both)
    limits = jnp.tile(both, (1, GROUP))[:, None, :]
    reqs = jnp.broadcast_to(jnp.where(row_ids == 0, my_req, other_req)[:, None], (8, HD))
    vmem = pl.BlockSpec(memory_space=pltpu.VMEM)
    dma = pltpu.SemaphoreType.DMA
    return pl.pallas_call(
        functools.partial(whole_kernel, n_shard, 1.0 / math.sqrt(HD)),
        out_shape=jax.ShapeDtypeStruct(queries.shape, jnp.bfloat16),
        in_specs=[pl.BlockSpec(memory_space=pltpu.SMEM)] + [vmem] * 10,
        out_specs=vmem,
        scratch_shapes=[
            pltpu.VMEM((heads, peers, block_len, 2 * HD), jnp.bfloat16),
            pltpu.VMEM((heads, peers, block_len, 2 * HD), jnp.bfloat16),
            pltpu.VMEM((peers, 8, HD), jnp.int32),
            pltpu.VMEM((heads, rows, GROUP * HD), jnp.bfloat16),
            pltpu.VMEM((2, lanes, HD), jnp.bfloat16),
            pltpu.VMEM((2, 1, lanes), jnp.float32),
            pltpu.VMEM((2, 1, lanes), jnp.float32),
            pltpu.VMEM((2, HD, lanes), jnp.float32),
            pltpu.VMEM((heads, HD, lanes), jnp.float32),
            pltpu.VMEM((heads, 1, lanes), jnp.float32),
            pltpu.VMEM((heads, HD, lanes), jnp.bfloat16),
            pltpu.VMEM((heads, GROUP, rows), jnp.float32),
            pltpu.VMEM((heads, HD, lanes), jnp.bfloat16),
            pltpu.VMEM((heads, GROUP, rows), jnp.float32),
            dma((heads, peers)),
            dma((heads, peers)),
            dma((peers,)),
            dma((peers,)),
            dma((heads,)),
            dma((heads,)),
            dma((heads,)),
            dma((heads,)),
            dma((heads,)),
            dma((heads,)),
            dma((heads + 1,)),
        ],
        compiler_params=pltpu.CompilerParams(
            collective_id=0, has_side_effects=True, vmem_limit_bytes=44 << 20
        ),
        cost_estimate=pl.CostEstimate(
            flops=4 * heads * peers * block_len * lanes * HD,
            bytes_accessed=8 << 20,
            transcendentals=heads * peers * block_len * lanes,
        ),
        name="whole",
    )(sel, kv_store, block_cos, block_sin, meta, queries, fresh_rows, row_cos, row_sin, limits, reqs)


def solution(mesh):
    in_specs = (
        P(("groups", "shard"), None, None),
        P(("groups", "shard")),
        P("groups"),
        P("groups", None),
        P("groups", "shard"),
        P("groups", "shard"),
    )
    out_specs = P("groups", "shard")
    return jax.shard_map(shards, mesh=mesh, in_specs=in_specs, out_specs=out_specs, check_vma=False)
```

profile of v0, /device:TPU:1, one launch (start us, length us, event | category | flops | bytes accessed | tf_op | source)
XLA Modules:
  0.0 113.6 jit_solution(1733513721086530944)
XLA Ops:
  0.0 0.8 constant_dynamic-slice_fusion
  0.8 0.8 select_reduce_fusion
  1.6 0.1 slice.3
  1.6 0.8 fusion.1
  2.5 0.2 fusion.2
  2.7 0.7 and_select_fusion
  3.3 0.1 select_reduce_fusion.2
  3.4 0.1 broadcast_select_fusion
  3.5 0.1 fusion.5
  3.6 0.1 pad_maximum_fusion.3.bsin_ref
  3.7 0.1 pad_maximum_fusion.2.bcos_ref
  3.8 0.1 broadcast_in_dim.122.req_ref
  3.9 0.1 broadcast_in_dim.119.meta_ref
  3.9 0.5 fusion
  4.5 0.1 pad_maximum_fusion
  4.6 0.0 copy-start
  4.6 1.6 %copy-done = bf16[2,256,2048]{2,1,0:T(8,128)(2,1)S(1)} copy-done((bf16[2,256,2048]{2,1,0:T(8,128)(2,1)S(1)}, bf16[2,256,2048]{2,1,0:T(8,128)(2,1)}, u32[]{:S(2)}) %copy-start) | copy-done | bytes 2097176
  6.2 0.0 copy-start.1
  6.2 1.2 %copy-done.1 = bf16[128,4096]{1,0:T(8,128)(2,1)S(1)} copy-done((bf16[128,4096]{1,0:T(8,128)(2,1)S(1)}, bf16[128,4096]{1,0:T(8,128)(2,1)}, u32[]{:S(2)}) %copy-start.1) | copy-done | bytes 1048600
  7.4 0.0 copy-start.2
  7.4 0.9 copy-done.2
  8.4 104.2 %whole.1 = bf16[128,4096]{1,0:T(8,128)(2,1)S(1)} custom-call(s32[4]{0:T(128)S(1)} %get-tuple-element.7.sel_ref, bf16[2,256,2048]{2,1,0:T(8,128)(2,1)S(1)} %copy-done, f32[2,1,128]{2,1,0:T(1,128)S(1)} %pad_maximum_fusion.2.bcos_ref, f32[2,1,128]{2,1,0:T(1,128)S(1)} %pad_maximum_fusion.3.bsin_ref, s32[4,8,128]{2,1,0:T(8,128)S(1)} %broadcast_in_dim.119.meta_ref, ...), custom_call_target="tpu_custom_call" | custom-call | flops 4294967296 | bytes 8388608 | tf_op jit(solution)/shard_map/whole/pallas_call | solution.py:341
  112.6 1.0 copy.8
  (6 shorter events, 0.0 us)
Async XLA Ops:
  4.6 1.6 %copy-start = (bf16[2,256,2048]{2,1,0:T(8,128)(2,1)S(1)}, bf16[2,256,2048]{2,1,0:T(8,128)(2,1)}, u32[]{:S(2)}) copy-start(bf16[2,256,2048]{2,1,0:T(8,128)(2,1)} %kv_ref.1) | copy-start | bytes 6291460
  6.2 1.2 %copy-start.1 = (bf16[128,4096]{1,0:T(8,128)(2,1)S(1)}, bf16[128,4096]{1,0:T(8,128)(2,1)}, u32[]{:S(2)}) copy-start(bf16[128,4096]{1,0:T(8,128)(2,1)} %q_ref.1) | copy-start | bytes 3145732
  7.4 0.9 copy-start.2
where the time goes:
time: 114 us
  Pallas kernels  104 us (91%)
  local copies, waits for them, and re-layouts  5.71 us (5%)
  other arithmetic  3.6 us (3%)
    pallas_call x1, Pallas kernels, shards(): pl.pallas_call(functools.partial(whole_kernel, n_shard, 1.0 / math.sqrt(H...  104 us
    unnamed x7, local copies, waits for them, and re-layouts  4.73 us

commit v1 on v0

--- a/solution.py
+++ b/solution.py
@@ -23,18 +23,16 @@
 TN = (((0,), (0,)), ((), ()))
 
 
-def frequencies(half_size):
-    step_ids = jnp.arange(half_size, dtype=jnp.float32)
-    return jnp.exp(-math.log(ROPE_BASE) * step_ids / half_size)
+def frequency_lanes():
+    lane = lax.rem(lax.broadcasted_iota(jnp.int32, (1, HD), 1), HD // 2)
+    return jnp.exp(-math.log(ROPE_BASE) * lane.astype(jnp.float32) / (HD // 2))
 
 
 def turn_tables(positions):
-    angle = positions.astype(jnp.float32)[..., None] * frequencies(HD // 2)
-    cosine, sine = jnp.cos(angle), jnp.sin(angle)
-    return (
-        jnp.concatenate([cosine, cosine], axis=-1),
-        jnp.concatenate([-sine, sine], axis=-1),
-    )
+    angle = positions.astype(jnp.float32) * frequency_lanes()
+    lower = lax.broadcasted_iota(jnp.int32, angle.shape, 1) < HD // 2
+    sine = jnp.sin(angle)
+    return jnp.cos(angle), jnp.where(lower, -sine, sine)
 
 
 def turned(x, cosine, sine):
@@ -42,25 +40,25 @@
     return (x * cosine + pltpu.roll(x, HD // 2, 1) * sine).astype(jnp.bfloat16)
 
 
-def lookup(values, table_ids, where_at):
-    return jnp.sum(jnp.where(where_at[..., None] == table_ids, values, 0), axis=-1)
-
-
 def whole_kernel(
     n,
     scale,
+    order_ref,
+    lengths_ref,
+    positions_ref,
+    kv_hbm,
+    q_hbm,
+    fresh_hbm,
+    out_ref,
+    kv_ref,
+    q_ref,
+    fresh_ref,
     sel_ref,
-    kv_ref,
     bcos_ref,
     bsin_ref,
     meta_ref,
-    q_ref,
-    fresh_ref,
     cos_ref,
     sin_ref,
-    limit_ref,
-    req_ref,
-    out_ref,
     sent,
     received,
     metas,
@@ -86,6 +84,7 @@
     l_send,
     l_recv,
     local_sem,
+    load_sem,
 ):
     heads, peers, block_len, _ = sent.shape
     rows = q_ref.shape[0]
@@ -118,7 +117,7 @@
 
     def q_copy(c):
         columns = pl.ds(pl.multiple_of(c * q_width, q_width), q_width)
-        return remote(q_ref.at[:, columns], partner_q.at[c], q_send.at[c], q_recv.at[c], partner)
+        return remote(q_hbm.at[:, columns], partner_q.at[c], q_send.at[c], q_recv.at[c], partner)
 
     def o_copy(c):
         return remote(o1.at[c], o1_in.at[c], o_send.at[c], o_recv.at[c], partner)
@@ -128,6 +127,13 @@
 
     def own_kv(c):
         return pltpu.make_async_copy(sent.at[c, me], received.at[c, me], local_sem.at[c])
+
+    loads = [
+        pltpu.make_async_copy(hbm, here, load_sem.at[i])
+        for i, (hbm, here) in enumerate(((kv_hbm, kv_ref), (q_hbm, q_ref), (fresh_hbm, fresh_ref)))
+    ]
+    for load in loads:
+        load.start()
 
     barrier = pltpu.get_barrier_semaphore()
     pl.semaphore_signal(barrier, inc=1, device_id={"shard": partner}, device_id_type=pl.DeviceIdType.MESH)
@@ -142,7 +148,37 @@
         return carry
 
     lax.fori_loop(1, peers, greet, 0)
+    my_req = device // per_req
+    other_req = lax.rem(my_req + PAIRS, REQS)
+    reqs, offsets = [], []
+    for b in range(order_ref.shape[0]):
+        block = order_ref[b]
+        start, req, own_start = jnp.int32(0), jnp.int32(-1), jnp.int32(0)
+        for r in range(REQS):
+            inside = block >= start
+            req = jnp.where(inside, r, req)
+            own_start = jnp.where(inside, start, own_start)
+            start = start + lengths_ref[r]
+        offset = (block - own_start) * block_len
+        reqs.append(req)
+        offsets.append(offset)
+        cosine, sine = turn_tables(jnp.full((1, HD), offset, jnp.int32))
+        bcos_ref[b] = cosine
+        bsin_ref[b] = sine
+    row_of_8 = lax.broadcasted_iota(jnp.int32, (8, HD), 0)
+    for p in range(PAIRS):
+        sel, pair_req, pair_offset = jnp.int32(0), jnp.int32(-1), jnp.int32(0)
+        for b, (req, offset) in enumerate(zip(reqs, offsets)):
+            match = lax.rem(req, PAIRS) == p
+            sel = jnp.where(match, b, sel)
+            pair_req = jnp.where(match, req, pair_req)
+            pair_offset = jnp.where(match, offset, pair_offset)
+        sel_ref[p] = sel
+        meta_ref[p] = jnp.where(row_of_8 == 0, pair_req, pair_offset)
+
     pl.semaphore_wait(barrier, peers)
+    q_copy(0).start()
+    loads[0].wait()
 
     own_meta = pltpu.make_async_copy(meta_ref.at[me // per_req], metas.at[me], local_sem.at[heads])
     own_meta.start()
@@ -154,7 +190,9 @@
     lax.fori_loop(1, peers, tell, 0)
 
     def pack_chunk(c, carry):
-        q_copy(c).start()
+        @pl.when(c > 0)
+        def _():
+            q_copy(c).start()
 
         def pack(t, carry):
             i = lax.rem(me + t, peers)
@@ -184,6 +222,16 @@
         meta_copy(j, j).wait_recv()
         return carry
 
+    limits = []
+    for side, req in enumerate((my_req, other_req)):
+        positions = positions_ref[pl.ds(req, 1), :]
+        limits.append(jnp.concatenate([positions] * GROUP, axis=1))
+        column = jnp.broadcast_to(positions.astype(jnp.float32), (HD, rows)).T
+        cosine, sine = turn_tables(column)
+        cos_ref[side] = cosine
+        sin_ref[side] = sine
+    loads[1].wait()
+    loads[2].wait()
     own_meta.wait()
     lax.fori_loop(1, peers, hear, 0)
 
@@ -221,15 +269,15 @@
 
             req = metas[j, 0:1, :]
             offset = metas[j, 1:2, :]
-            is_own = req == req_ref[0:1, :]
-            is_partner = req == req_ref[1:2, :]
+            is_own = req == my_req
+            is_partner = req == other_req
             pick0 = jnp.where(is_own, 1.0, 0.0).astype(jnp.bfloat16)
             pick1 = jnp.where(is_own, 0.0, 1.0).astype(jnp.bfloat16)
             query = qs[0] * pick0 + qs[1] * pick1
             wide_own = jnp.concatenate([is_own.astype(jnp.int32)] * GROUP, axis=1) > 0
             wide_partner = jnp.concatenate([is_partner.astype(jnp.int32)] * GROUP, axis=1) > 0
             wide_offset = jnp.concatenate([offset] * GROUP, axis=1)
-            limit = jnp.where(wide_own, limit_ref[0], limit_ref[1]) - wide_offset
+            limit = jnp.where(wide_own, limits[0], limits[1]) - wide_offset
             keys = received[c, j, :, pl.ds(0, HD)]
             values = received[c, j, :, pl.ds(HD, HD)]
             scores = lax.dot_general(keys, query, NT, preferred_element_type=jnp.float32)
@@ -310,40 +358,25 @@
     heads = width // (per_req * 2 * HD)
     rows = queries.shape[0]
     lanes = rows * GROUP
-    my_req = lax.axis_index("shard") // per_req
-    req_ids = jnp.arange(REQS, dtype=jnp.int32)
-    starts = jnp.sum(jnp.where(req_ids[None, :] < req_ids[:, None], lengths[None, :], 0), axis=1)
-    dest = jnp.sum((block_order[:, None] >= starts[None, 1:]).astype(jnp.int32), axis=-1)
-    offset = (block_order - lookup(starts, req_ids, dest)) * block_len
-    pair_ids = jnp.arange(PAIRS, dtype=jnp.int32)
-    slot_ids = jnp.arange(blk_dev, dtype=jnp.int32)
-    for_pair = (dest % PAIRS)[None, :] == pair_ids[:, None]
-    sel = jnp.sum(jnp.where(for_pair, slot_ids[None, :], 0), axis=1)
-    pair_req = jnp.sum(jnp.where(for_pair, dest[None, :] + 1, 0), axis=1) - 1
-    pair_offset = jnp.sum(jnp.where(for_pair, offset[None, :], 0), axis=1)
-    row_ids = jnp.arange(8, dtype=jnp.int32)
-    meta = jnp.broadcast_to(
-        jnp.where(row_ids[None, :] == 0, pair_req[:, None], pair_offset[:, None])[:, :, None], (PAIRS, 8, HD)
-    )
-    block_cos, block_sin = turn_tables(offset[:, None])
-    other_req = (my_req + PAIRS) % REQS
-    both = jnp.stack(
-        [
-            lax.dynamic_index_in_dim(row_positions, my_req, 0, keepdims=False),
-            lax.dynamic_index_in_dim(row_positions, other_req, 0, keepdims=False),
-        ]
-    )
-    row_cos, row_sin = turn_tables(both)
-    limits = jnp.tile(both, (1, GROUP))[:, None, :]
-    reqs = jnp.broadcast_to(jnp.where(row_ids == 0, my_req, other_req)[:, None], (8, HD))
     vmem = pl.BlockSpec(memory_space=pltpu.VMEM)
+    smem = pl.BlockSpec(memory_space=pltpu.SMEM)
+    anywhere = pl.BlockSpec(memory_space=pl.ANY)
     dma = pltpu.SemaphoreType.DMA
     return pl.pallas_call(
         functools.partial(whole_kernel, n_shard, 1.0 / math.sqrt(HD)),
         out_shape=jax.ShapeDtypeStruct(queries.shape, jnp.bfloat16),
-        in_specs=[pl.BlockSpec(memory_space=pltpu.SMEM)] + [vmem] * 10,
+        in_specs=[smem, smem, vmem, anywhere, anywhere, anywhere],
         out_specs=vmem,
         scratch_shapes=[
+            pltpu.VMEM(kv_store.shape, kv_store.dtype),
+            pltpu.VMEM(queries.shape, queries.dtype),
+            pltpu.VMEM(fresh_rows.shape, fresh_rows.dtype),
+            pltpu.SMEM((PAIRS,), jnp.int32),
+            pltpu.VMEM((blk_dev, 1, HD), jnp.float32),
+            pltpu.VMEM((blk_dev, 1, HD), jnp.float32),
+            pltpu.VMEM((PAIRS, 8, HD), jnp.int32),
+            pltpu.VMEM((2, rows, HD), jnp.float32),
+            pltpu.VMEM((2, rows, HD), jnp.float32),
             pltpu.VMEM((heads, peers, block_len, 2 * HD), jnp.bfloat16),
             pltpu.VMEM((heads, peers, block_len, 2 * HD), jnp.bfloat16),
             pltpu.VMEM((peers, 8, HD), jnp.int32),
@@ -369,9 +402,10 @@
             dma((heads,)),
             dma((heads,)),
             dma((heads + 1,)),
+            dma((3,)),
         ],
         compiler_params=pltpu.CompilerParams(
-            collective_id=0, has_side_effects=True, vmem_limit_bytes=44 << 20
+            collective_id=0, has_side_effects=True, vmem_limit_bytes=60 << 20
         ),
         cost_estimate=pl.CostEstimate(
             flops=4 * heads * peers * block_len * lanes * HD,
@@ -379,7 +413,7 @@
             transcendentals=heads * peers * block_len * lanes,
         ),
         name="whole",
-    )(sel, kv_store, block_cos, block_sin, meta, queries, fresh_rows, row_cos, row_sin, limits, reqs)
+    )(block_order, lengths, row_positions, kv_store, queries, fresh_rows)
 
 
 def solution(mesh):

time: 114 us -> 108 us (0.947)
  other arithmetic: 3.6 us -> 0 us
  local copies, waits for them, and re-layouts: 5.71 us -> 2.29 us
  Pallas kernels: 104 us -> 106 us
    unnamed x7 -> x1, local copies, waits for them, and re-layouts: 4.73 us -> 2.29 us
    reduce_sum x4 -> x0, other arithmetic: 1.89 us -> none  [the longest x1 0.84 us: shards(): jnp.sum((block_order[:, None] >= starts[None, 1:]).astype(jnp.int32), axi...]
    pallas_call x1, Pallas kernels: 104 us -> 106 us  [shards(): pl.pallas_call(functools.partial(whole_kernel, n_shard, 1.0 / math.sqrt(H...]
where the time goes in v1:
time: 108 us
  Pallas kernels  106 us (98%)
  local copies, waits for them, and re-layouts  2.29 us (2%)
    pallas_call x1, Pallas kernels, shards(): pl.pallas_call(functools.partial(whole_kernel, n_shard, 1.0 / math.sqrt(H...  106 us
    unnamed x1, local copies, waits for them, and re-layouts  2.29 us

profile of v1, /device:TPU:1, one launch (start us, length us, event | category | flops | bytes accessed | tf_op | source)
XLA Modules:
  0.0 107.9 jit_solution(14436003899118531450)
XLA Ops:
  0.0 105.6 %whole.1 = bf16[128,4096]{1,0:T(8,128)(2,1)} custom-call(s32[2]{0:T(128)} %order_ref.1, s32[8]{0:T(128)} %lengths_ref.1, s32[8,128]{1,0:T(8,128)} %positions_ref.1, bf16[2,256,2048]{2,1,0:T(8,128)(2,1)} %kv_hbm.1, bf16[128,4096]{1,0:T(8,128)(2,1)} %q_hbm.1, bf16[128,1024]{1,0:T(8,128)(2,1)} %fresh_hbm.1), custom_call_target="tpu_custom_call" | custom-call | flops 4294967296 | bytes 8388608 | tf_op jit(solution)/shard_map/whole/pallas_call | solution.py:365
  105.6 2.3 %copy.8 = bf16[128,4096]{1,0:T(8,128)(2,1)} copy(bf16[128,4096]{1,0:T(8,128)(2,1)} %whole.1) | data formatting | bytes 2097152

commit v2 on v1

--- a/solution.py
+++ b/solution.py
@@ -148,6 +148,13 @@
         return carry
 
     lax.fori_loop(1, peers, greet, 0)
+    pl.semaphore_wait(barrier, peers)
+
+    def ask(c, carry):
+        q_copy(c).start()
+        return carry
+
+    lax.fori_loop(0, heads, ask, 0)
     my_req = device // per_req
     other_req = lax.rem(my_req + PAIRS, REQS)
     reqs, offsets = [], []
@@ -176,8 +183,6 @@
         sel_ref[p] = sel
         meta_ref[p] = jnp.where(row_of_8 == 0, pair_req, pair_offset)
 
-    pl.semaphore_wait(barrier, peers)
-    q_copy(0).start()
     loads[0].wait()
 
     own_meta = pltpu.make_async_copy(meta_ref.at[me // per_req], metas.at[me], local_sem.at[heads])
@@ -190,10 +195,6 @@
     lax.fori_loop(1, peers, tell, 0)
 
     def pack_chunk(c, carry):
-        @pl.when(c > 0)
-        def _():
-            q_copy(c).start()
-
         def pack(t, carry):
             i = lax.rem(me + t, peers)
             pair, group = i // per_req, lax.rem(i, per_req)

time: 108 us -> 108 us (level)
  no operation moved by 1% of the time
where the time goes in v2:
time: 108 us
  Pallas kernels  105 us (97%)
  local copies, waits for them, and re-layouts  2.29 us (2%)
    pallas_call x1, Pallas kernels, shards(): pl.pallas_call(functools.partial(whole_kernel, n_shard, 1.0 / math.sqrt(H...  105 us
    unnamed x1, local copies, waits for them, and re-layouts  2.29 us

profile of v2, /device:TPU:1, one launch (start us, length us, event | category | flops | bytes accessed | tf_op | source)
XLA Modules:
  0.0 107.7 jit_solution(4531657060872542882)
XLA Ops:
  0.0 105.4 %whole.1 = bf16[128,4096]{1,0:T(8,128)(2,1)} custom-call(s32[2]{0:T(128)} %order_ref.1, s32[8]{0:T(128)} %lengths_ref.1, s32[8,128]{1,0:T(8,128)} %positions_ref.1, bf16[2,256,2048]{2,1,0:T(8,128)(2,1)} %kv_hbm.1, bf16[128,4096]{1,0:T(8,128)(2,1)} %q_hbm.1, bf16[128,1024]{1,0:T(8,128)(2,1)} %fresh_hbm.1), custom_call_target="tpu_custom_call" | custom-call | flops 4294967296 | bytes 8388608 | tf_op jit(solution)/shard_map/whole/pallas_call | solution.py:366
  105.4 2.3 %copy.8 = bf16[128,4096]{1,0:T(8,128)(2,1)} copy(bf16[128,4096]{1,0:T(8,128)(2,1)} %whole.1) | data formatting | bytes 2097152

commit v3 on v2

--- a/solution.py
+++ b/solution.py
@@ -154,7 +154,7 @@
         q_copy(c).start()
         return carry
 
-    lax.fori_loop(0, heads, ask, 0)
+    lax.fori_loop(0, min(2, heads), ask, 0)
     my_req = device // per_req
     other_req = lax.rem(my_req + PAIRS, REQS)
     reqs, offsets = [], []
@@ -238,6 +238,11 @@
 
     def attend_chunk(c, carry):
         q_copy(c).wait_recv()
+
+        @pl.when(c + 2 < heads)
+        def _():
+            q_copy(c + 2).start()
+
         f_column = pl.multiple_of(c * 2 * HD, 2 * HD)
         for g in range(GROUP):
             own_rows = pl.ds(g * rows, rows)

time: 108 us -> 116 us (1.074)
  Pallas kernels: 105 us -> 113 us
    pallas_call x1, Pallas kernels: 105 us -> 113 us  [shards(): pl.pallas_call(functools.partial(whole_kernel, n_shard, 1.0 / math.sqrt(H...]
where the time goes in v3:
time: 116 us; the launch traced here: 115 us
  Pallas kernels  113 us (97%)
  local copies, waits for them, and re-layouts  2.29 us (2%)
    pallas_call x1, Pallas kernels, shards(): pl.pallas_call(functools.partial(whole_kernel, n_shard, 1.0 / math.sqrt(H...  113 us

profile of v3, /device:TPU:1, one launch (start us, length us, event | category | flops | bytes accessed | tf_op | source)
XLA Modules:
  0.0 115.2 jit_solution(8285456101467218418)
XLA Ops:
  0.0 112.9 %whole.1 = bf16[128,4096]{1,0:T(8,128)(2,1)} custom-call(s32[2]{0:T(128)} %order_ref.1, s32[8]{0:T(128)} %lengths_ref.1, s32[8,128]{1,0:T(8,128)} %positions_ref.1, bf16[2,256,2048]{2,1,0:T(8,128)(2,1)} %kv_hbm.1, bf16[128,4096]{1,0:T(8,128)(2,1)} %q_hbm.1, bf16[128,1024]{1,0:T(8,128)(2,1)} %fresh_hbm.1), custom_call_target="tpu_custom_call" | custom-call | flops 4294967296 | bytes 8388608 | tf_op jit(solution)/shard_map/whole/pallas_call | solution.py:371
  112.9 2.3 %copy.8 = bf16[128,4096]{1,0:T(8,128)(2,1)} copy(bf16[128,4096]{1,0:T(8,128)(2,1)} %whole.1) | data formatting | bytes 2097152
